TPU v7x, 32 devices: a whole 2x2x4 slice. The times are simulated.
32 devices in a mesh: parts: 2 (over y), lat: 4 (over z), lon: 2 (over x), rep: 2 (over core).
Axes of the slice: x: 2, y: 2, z: 4, core: 2. Of those that a mesh axis runs over, the one named last changes fastest.
Arguments:
- observations: bfloat16 [1024, 256], P(('parts', 'lat', 'lon'), 'rep'), parts along dimension 0, may hold values from -6 to 6
- send_counts: int32 [16, 8], P(('parts', 'lat', 'lon')), parts along dimension 0, may hold values from 0 to 8, as said below
- bucket_slots: int32 [16, 8, 8], P(('parts', 'lat', 'lon')), parts along dimension 0, may hold values from 0 to 1024, as said below
- latent: bfloat16 [64, 64, 768], P(('parts', 'lat'), 'lon'), parts along dimension 0, may hold values from -6 to 6
- norm_gain: float32 [768], replicated, may hold values from 0.25 to 1.75
- w_query: bfloat16 [768, 768], P(None, 'rep'), may hold values from -0.21875 to 0.21875
- w_key: bfloat16 [256, 768], P(None, 'rep'), may hold values from -0.375 to 0.375
- w_value: bfloat16 [256, 768], P(None, 'rep'), may hold values from -0.375 to 0.375
- null_kv: bfloat16 [2, 768], P(None, 'rep'), may hold values from -8 to 8
- rel_bias: float32 [12, 25], P('rep')
- w_out: bfloat16 [768, 768], P('rep'), may hold values from -0.21875 to 0.21875
- w_up: bfloat16 [3072, 768], P(('lat', 'rep')), may hold values from -0.21875 to 0.21875
- w_down: bfloat16 [3072, 768], P(('lat', 'rep')), may hold values from -0.109375 to 0.109375
Outputs:
- updated: bfloat16 [64, 64, 768], P(('parts', 'lat', 'rep'), 'lon'), parts along dimension 0
There are 2 independent parts, one for each index of `parts`. A program takes and returns all parts, laid end to end along the dimension named above; an argument that names none is the same for every part. Nothing has to cross between parts.
Inputs may be any that keep to these rules, and one draw needn't show every extreme that they name: `send_counts`: for each source the counts sum to at most 64; every source s sends 8 rows to owner s and to owner (s + 1) mod 8, and none to some other owner. `bucket_slots`: for owner d and source s, entry k is a slot below 1024 exactly when k < send_counts[s, d], and 1024 otherwise; the slots below 1024 of one owner are all different. `observations`: every row has a nonzero channel in each of its halves along the channels.
All inputs are finite; a program needn't handle non-finite values.
Results may differ from a plain program's by a relative error of at most 0.0054.
Values may be sent and summed in bfloat16 or wider, within the bound.
A program may use at most 192 MiB of HBM per device.

v0:
```python
import math

import jax
import jax.numpy as jnp
from jax import lax
from jax.sharding import PartitionSpec as P

HEAD = 64
BUCKET = 4
REACH = 2


def extended(cells, sides, width):
    for axis, dim in sides:
        count = lax.axis_size(axis)
        head = lax.slice_in_dim(cells, 0, width, axis=dim)
        tail = lax.slice_in_dim(cells, cells.shape[dim] - width, cells.shape[dim], axis=dim)
        cells = jnp.concatenate(
            [
                lax.ppermute(tail, axis, [(i, (i + 1) % count) for i in range(count)]),
                cells,
                lax.ppermute(head, axis, [((i + 1) % count, i) for i in range(count)]),
            ],
            axis=dim,
        )
    return cells


def local(
    observations,
    send_counts,
    bucket_slots,
    latent,
    norm_gain,
    w_query,
    w_key,
    w_value,
    null_kv,
    rel_bias,
    w_out,
    w_up,
    w_down,
):
    counts = send_counts[0]
    places = bucket_slots.shape[2]
    half_chan = observations.shape[1]
    offsets = jnp.cumsum(counts) - counts
    within = jnp.arange(places, dtype=jnp.int32)
    active = within[None, :] < counts[:, None]
    picked = jnp.where(active, offsets[:, None] + within[None, :], 0)
    packed = jnp.where(active[:, :, None], observations[picked], jnp.zeros((), jnp.bfloat16))
    arrived = lax.all_to_all(packed, ("lat", "lon"), split_axis=0, concat_axis=0, tiled=True)
    lat_cells = latent.shape[0]
    lon_cells = latent.shape[1]
    slot_total = lat_cells * lon_cells * BUCKET
    target = bucket_slots[0].reshape(-1)
    slot_rows = (
        jnp.zeros((slot_total + 1, half_chan), jnp.bfloat16)
        .at[target]
        .set(arrived.reshape(-1, half_chan))
    )
    buckets = slot_rows[:slot_total].reshape(lat_cells, lon_cells, BUCKET, half_chan)
    rows_ext = lax.axis_index("lat") * lat_cells + jnp.arange(
        -REACH, lat_cells + REACH, dtype=jnp.int32
    )
    inside = (rows_ext >= 0) & (rows_ext < lat_cells * lax.axis_size("lat"))
    padded = extended(buckets, (("lat", 0), ("lon", 1)), REACH)
    padded = jnp.where(inside[:, None, None, None], padded, jnp.zeros((), jnp.bfloat16))
    widened = lax.all_gather(padded, "rep", axis=3, tiled=True)
    keys_ext = jnp.dot(widened, w_key, preferred_element_type=jnp.float32).astype(jnp.bfloat16)
    values_ext = jnp.dot(widened, w_value, preferred_element_type=jnp.float32).astype(jnp.bfloat16)
    filled_ext = jnp.any(widened != 0, axis=-1)
    lat_float = latent.astype(jnp.float32)
    inv_rms = lax.rsqrt(jnp.mean(lat_float * lat_float, axis=-1, keepdims=True) + 1e-06)
    normed = (lat_float * inv_rms * norm_gain).astype(jnp.bfloat16)
    queries = jnp.dot(normed, w_query, preferred_element_type=jnp.float32).astype(jnp.bfloat16)
    heads_here = w_query.shape[1] // HEAD
    window_side = 2 * REACH + 1
    wide_cols = lon_cells + 2 * REACH
    query_heads = queries.reshape(lat_cells, lon_cells, heads_here, HEAD)
    key_heads = keys_ext.reshape(lat_cells + 2 * REACH, wide_cols, BUCKET, heads_here, HEAD)
    value_heads = values_ext.reshape(lat_cells + 2 * REACH, wide_cols, BUCKET, heads_here, HEAD)
    null_key = null_kv[0].reshape(heads_here, HEAD)
    null_value = null_kv[1].astype(jnp.float32).reshape(heads_here, HEAD)
    score_scale = 1.0 / math.sqrt(HEAD)
    null_scores = (
        jnp.einsum("yxhe,he->hyx", query_heads, null_key, preferred_element_type=jnp.float32)
        * score_scale
    )
    score_parts = [null_scores[..., None]]
    for row_step in range(window_side):
        for col_step in range(window_side):
            place = row_step * window_side + col_step
            window_keys = key_heads[
                row_step : row_step + lat_cells, col_step : col_step + lon_cells
            ]
            local_scores = (
                jnp.einsum(
                    "yxhe,yxbhe->hyxb", query_heads, window_keys, preferred_element_type=jnp.float32
                )
                * score_scale
            )
            local_scores = local_scores + rel_bias[:, place][:, None, None, None]
            window_mask = filled_ext[
                row_step : row_step + lat_cells, col_step : col_step + lon_cells
            ]
            score_parts.append(jnp.where(window_mask[None], local_scores, -jnp.inf))
    scores = jnp.concatenate(score_parts, axis=-1)
    row_max = jnp.max(scores, axis=-1, keepdims=True)
    exponent = jnp.exp(scores - row_max)
    weights = (exponent / jnp.sum(exponent, axis=-1, keepdims=True)).astype(jnp.bfloat16)
    null_share = jnp.transpose(weights[..., 0], (1, 2, 0)).astype(jnp.float32)
    mixture = null_share[..., None] * null_value[None, None]
    for row_step in range(window_side):
        for col_step in range(window_side):
            place = row_step * window_side + col_step
            window_values = value_heads[
                row_step : row_step + lat_cells, col_step : col_step + lon_cells
            ]
            share = weights[..., 1 + place * BUCKET : 1 + (place + 1) * BUCKET]
            mixture = mixture + jnp.einsum(
                "hyxb,yxbhe->yxhe", share, window_values, preferred_element_type=jnp.float32
            )
    mixed = mixture.astype(jnp.bfloat16).reshape(lat_cells * lon_cells, heads_here * HEAD)
    attended = jnp.dot(mixed, w_out, preferred_element_type=jnp.float32)
    flat_normed = normed.reshape(lat_cells * lon_cells, -1)
    raised = lax.dot_general(
        flat_normed,
        lax.all_gather(w_up, "lat", axis=0, tiled=True),
        (((1,), (1,)), ((), ())),
        preferred_element_type=jnp.float32,
    )
    hidden = jax.nn.gelu(raised, approximate=True).astype(jnp.bfloat16)
    down_rows = lax.all_gather(w_down, "lat", axis=0, tiled=True)
    expanded = jnp.dot(hidden, down_rows, preferred_element_type=jnp.float32)
    combined = (attended + expanded).reshape(lat_cells, lon_cells, -1)
    summed = lax.psum_scatter(combined, "rep", scatter_dimension=0, tiled=True)
    share_rows = summed.shape[0]
    own_rows = lax.dynamic_slice_in_dim(
        lat_float, lax.axis_index("rep") * share_rows, share_rows, 0
    )
    return (own_rows + summed).astype(jnp.bfloat16)


def solution(mesh):
    in_specs = (
        P(("parts", "lat", "lon"), "rep"),
        P(("parts", "lat", "lon"), None),
        P(("parts", "lat", "lon"), None, None),
        P(("parts", "lat"), "lon", None),
        P(),
        P(None, "rep"),
        P(None, "rep"),
        P(None, "rep"),
        P(None, "rep"),
        P("rep", None),
        P("rep", None),
        P(("lat", "rep"), None),
        P(("lat", "rep"), None),
    )
    out_specs = P(("parts", "lat", "rep"), "lon", None)
    return jax.shard_map(local, mesh=mesh, in_specs=in_specs, out_specs=out_specs, check_vma=False)
```

profile of v0, /device:TPU:0, one launch (start us, length us, event | category | flops | bytes accessed | tf_op | source)
XLA Modules:
  0.0 414.2 jit_solution(3708053173727357713)
XLA Ops:
  12.3 7.3 %all-to-all-start = ((bf16[8,8,128]{2,1,0:T(8,128)(2,1)}), bf16[8,8,128]{2,1,0:T(8,128)(2,1)S(1)}, u32[]{:S(2)}, u32[]{:S(2)}) async-start(bf16[8,8,128]{2,1,0:T(8,128)(2,1)} %bitcast_select_fusion), calls=%async_computation | async-start | bytes 32768 | tf_op jit(solution)/shard_map/all_to_all | solution.py:52
  32.7 4.2 %collective-permute-done = bf16[2,32,4,128]{3,1,2,0:T(8,128)(2,1)S(1)} collective-permute-done((bf16[2,32,4,128]{3,1,2,0:T(8,128)(2,1)S(1)}, bf16[2,32,4,128]{3,1,2,0:T(8,128)(2,1)S(1)}, u32[]{:S(2)}, u32[]{:S(2)}) %collective-permute-start) | collective-permute-done | bytes 65568 | tf_op jit(solution)/shard_map/ppermute | solution.py:20
  49.9 3.6 reshape.317
  53.5 8.6 %fusion.232 = (bf16[8,32,4,6,64]{4,3,2,1,0:T(8,128)(2,1)}, bf16[8,32,4,6,64]{4,3,2,1,0:T(8,128)(2,1)}, bf16[8,32,4,6,64]{4,3,2,1,0:T(8,128)(2,1)}, bf16[8,32,4,6...) fusion(bf16[12,36,4,6,64]{4,3,2,1,0:T(8,128)(2,1)} %reshape.317), kind=kLoop, calls=%fused_computation.364 | loop fusion | bytes 9437184 | tf_op jit(solution)/shard_map/slice | solution.py:94
  62.1 13.4 %fusion.231 = (bf16[8,32,4,6,64]{4,3,2,1,0:T(8,128)(2,1)}, bf16[8,32,4,6,64]{4,3,2,1,0:T(8,128)(2,1)}, bf16[8,32,4,6,64]{4,3,2,1,0:T(8,128)(2,1)}, bf16[8,32,4,6...) fusion(bf16[12,36,4,6,64]{4,3,2,1,0:T(8,128)(2,1)S(1)} %copy-done.1), kind=kLoop, calls=%fused_computation.363 | loop fusion | bytes 29884416 | tf_op jit(solution)/shard_map/slice | solution.py:94
  91.6 3.4 fusion.101
  97.3 3.4 fusion.99
  102.9 3.4 fusion.97
  114.1 3.4 fusion.93
  125.3 3.4 fusion.89
  131.0 3.4 fusion.87
  136.6 3.4 fusion.85
  164.9 3.4 fusion.75
  170.5 3.4 fusion.73
  191.3 3.4 fusion.65
  195.4 3.4 fusion.63
  199.4 3.4 fusion.61
  204.1 3.4 fusion.59
  244.4 27.7 %fusion.229 = (bf16[8,32,4,6,64]{4,3,2,1,0:T(8,128)(2,1)}, bf16[8,32,4,6,64]{4,3,2,1,0:T(8,128)(2,1)}, bf16[8,32,4,6,64]{4,3,2,1,0:T(8,128)(2,1)}, bf16[8,32,4,6...) fusion(bf16[12,36,4,6,64]{4,3,2,1,0:T(8,128)(2,1)} %reshape.318), kind=kLoop, calls=%fused_computation.361 | loop fusion | bytes 29884416 | tf_op jit(solution)/shard_map/slice | solution.py:117
  272.2 5.2 %fusion.230 = (bf16[8,32,4,6,64]{4,3,2,1,0:T(8,128)(2,1)}, bf16[8,32,4,6,64]{4,3,2,1,0:T(8,128)(2,1)}, bf16[8,32,4,6,64]{4,3,2,1,0:T(8,128)(2,1)}, bf16[8,32,4,6...) fusion(bf16[12,36,4,6,64]{4,3,2,1,0:T(8,128)(2,1)S(1)} %copy-done.2), kind=kLoop, calls=%fused_computation.362 | loop fusion | bytes 9437184 | tf_op jit(solution)/shard_map/slice | solution.py:117
  324.4 3.5 fusion.57
  374.5 3.7 fusion.55
  393.4 4.0 fusion.110
  398.8 7.0 %reduce-scatter.2.cloned.1.call-done = f32[4,32,768]{2,1,0:T(8,128)} async-done(((f32[8,32,768]{2,1,0:T(8,128)}), f32[4,32,768]{2,1,0:T(8,128)}) %reduce-scatter.2.cloned.1.call-update) | async-done | bytes 393232 | tf_op jit(solution)/shard_map/reduce_scatter | solution.py:137
  (475 shorter events, 267.6 us)
Async XLA Ops:
  6.5 390.9 %copy-start = (bf16[384,768]{1,0:T(8,128)(2,1)S(1)}, bf16[384,768]{1,0:T(8,128)(2,1)}, u32[]{:S(2)}) copy-start(bf16[384,768]{1,0:T(8,128)(2,1)} %param.23) | copy-start | bytes 1769476
  6.5 386.8 %all-gather.3.cloned.1.call-start = ((), (), s32[]{:S(2)}) async-start(), calls=%async_computation.2 | async-start | bytes 2949120 | tf_op jit(solution)/shard_map/all_gather | solution.py:129
  12.3 15.5 %all-to-all-start = ((bf16[8,8,128]{2,1,0:T(8,128)(2,1)}), bf16[8,8,128]{2,1,0:T(8,128)(2,1)S(1)}, u32[]{:S(2)}, u32[]{:S(2)}) async-start(bf16[8,8,128]{2,1,0:T(8,128)(2,1)} %bitcast_select_fusion), calls=%async_computation | async-start | bytes 32768 | tf_op jit(solution)/shard_map/all_to_all | solution.py:52
  19.6 373.8 %all-gather.5.cloned.1.call-start = ((), (), s32[]{:S(2)}) async-start(), calls=%async_computation.3 | async-start | bytes 2949120 | tf_op jit(solution)/shard_map/all_gather | solution.py:134
  20.3 385.5 %reduce-scatter.2.cloned.1.call-start = ((), (), s32[]{:S(2)}) async-start(), calls=%async_computation.4 | async-start | bytes 1179648 | tf_op jit(solution)/shard_map/reduce_scatter | solution.py:137
  28.7 8.2 %collective-permute-start = (bf16[2,32,4,128]{3,1,2,0:T(8,128)(2,1)S(1)}, bf16[2,32,4,128]{3,1,2,0:T(8,128)(2,1)S(1)}, u32[]{:S(2)}, u32[]{:S(2)}) collective-permute-start(bf16[2,32,4,128]{3,1,2,0:T(8,128)(2,1)S(1)} %copy.87), channel_id=1, source_target_pairs={{0,4},{4,8},{8,12},{12,0},{1,5},{5,9},{9,13},{13,1},{2,6},{6,10},{... | collective-permute-start | bytes 196616 | tf_op jit(solution)/shard_map/ppermute | solution.py:20
  30.9 8.6 %collective-permute-start.1 = (bf16[2,32,4,128]{3,1,2,0:T(8,128)(2,1)S(1)}, bf16[2,32,4,128]{3,1,2,0:T(8,128)(2,1)S(1)}, u32[]{:S(2)}, u32[]{:S(2)}) collective-permute-start(bf16[2,32,4,128]{3,1,2,0:T(8,128)(2,1)S(1)} %copy.88), channel_id=1, source_target_pairs={{4,0},{8,4},{12,8},{0,12},{5,1},{9,5},{13,9},{1,13},{6,2},{10,6},{... | collective-permute-start | bytes 196616 | tf_op jit(solution)/shard_map/ppermute | solution.py:22
  39.6 4.8 %collective-permute-start.2 = (bf16[12,2,4,128]{3,1,2,0:T(2,128)(2,1)S(1)}, bf16[12,2,4,128]{3,1,2,0:T(2,128)(2,1)S(1)}, u32[]{:S(2)}, u32[]{:S(2)}) collective-permute-start(bf16[12,2,4,128]{3,1,2,0:T(2,128)(2,1)S(1)} %get-tuple-element.105), channel_id=1, source_target_pairs={{0,2},{2,0},{1,3},{3,1},{4,6},{6,4},{5,7},{7,5},{8,10},{10,8},{9,1... | collective-permute-start | bytes 73736 | tf_op jit(solution)/shard_map/ppermute | solution.py:20
  41.2 3.8 collective-permute-start.3
  207.4 20.6 %copy-start.79 = (f32[6,8,32,1,4]{2,1,0,4,3:T(8,128)S(1)}, f32[6,8,32,1,4]{2,1,0,4,3:T(8,128)}, u32[]{:S(2)}) copy-start(f32[6,8,32,1,4]{2,1,0,4,3:T(8,128)} %copy.152) | copy-start | bytes 73732
  207.5 21.3 %copy-start.78 = (f32[6,8,32,1,4]{2,1,0,4,3:T(8,128)S(1)}, f32[6,8,32,1,4]{2,1,0,4,3:T(8,128)}, u32[]{:S(2)}) copy-start(f32[6,8,32,1,4]{2,1,0,4,3:T(8,128)} %copy.154) | copy-start | bytes 73732
  207.5 22.0 %copy-start.77 = (f32[6,8,32,1,4]{2,1,0,4,3:T(8,128)S(1)}, f32[6,8,32,1,4]{2,1,0,4,3:T(8,128)}, u32[]{:S(2)}) copy-start(f32[6,8,32,1,4]{2,1,0,4,3:T(8,128)} %copy.156) | copy-start | bytes 73732
  208.2 21.3 %copy-start.109 = (pred[8,32,4]{1,0,2:T(8,128)(4,1)S(1)}, pred[8,32,4]{1,0,2:T(8,128)(4,1)}, u32[]{:S(2)}) copy-start(pred[8,32,4]{1,0,2:T(8,128)(4,1)} %copy.107) | copy-start | bytes 3076
  208.3 21.3 %copy-start.126 = (f32[6]{0:T(128)S(1)}, f32[6]{0:T(128)}, u32[]{:S(2)}) copy-start(f32[6]{0:T(128)} %get-tuple-element.12) | copy-start | bytes 76
  208.3 22.0 %copy-start.76 = (f32[6,8,32,1,4]{2,1,0,4,3:T(8,128)S(1)}, f32[6,8,32,1,4]{2,1,0,4,3:T(8,128)}, u32[]{:S(2)}) copy-start(f32[6,8,32,1,4]{2,1,0,4,3:T(8,128)} %copy.158) | copy-start | bytes 73732
  208.3 22.0 %copy-start.108 = (pred[8,32,4]{1,0,2:T(8,128)(4,1)S(1)}, pred[8,32,4]{1,0,2:T(8,128)(4,1)}, u32[]{:S(2)}) copy-start(pred[8,32,4]{1,0,2:T(8,128)(4,1)} %copy.108) | copy-start | bytes 3076
  208.3 22.0 %copy-start.125 = (f32[6]{0:T(128)S(1)}, f32[6]{0:T(128)}, u32[]{:S(2)}) copy-start(f32[6]{0:T(128)} %get-tuple-element.11) | copy-start | bytes 76
  208.3 22.7 %copy-start.75 = (f32[6,8,32,1,4]{2,1,0,4,3:T(8,128)S(1)}, f32[6,8,32,1,4]{2,1,0,4,3:T(8,128)}, u32[]{:S(2)}) copy-start(f32[6,8,32,1,4]{2,1,0,4,3:T(8,128)} %copy.160) | copy-start | bytes 73732
  208.3 22.7 %copy-start.107 = (pred[8,32,4]{1,0,2:T(8,128)(4,1)S(1)}, pred[8,32,4]{1,0,2:T(8,128)(4,1)}, u32[]{:S(2)}) copy-start(pred[8,32,4]{1,0,2:T(8,128)(4,1)} %copy.109) | copy-start | bytes 3076
  208.3 22.6 %copy-start.124 = (f32[6]{0:T(128)S(1)}, f32[6]{0:T(128)}, u32[]{:S(2)}) copy-start(f32[6]{0:T(128)} %get-tuple-element.10) | copy-start | bytes 76
  210.7 21.0 %copy-start.74 = (f32[6,8,32,1,4]{2,1,0,4,3:T(8,128)S(1)}, f32[6,8,32,1,4]{2,1,0,4,3:T(8,128)}, u32[]{:S(2)}) copy-start(f32[6,8,32,1,4]{2,1,0,4,3:T(8,128)} %copy.162) | copy-start | bytes 73732
  210.7 21.0 %copy-start.106 = (pred[8,32,4]{1,0,2:T(8,128)(4,1)S(1)}, pred[8,32,4]{1,0,2:T(8,128)(4,1)}, u32[]{:S(2)}) copy-start(pred[8,32,4]{1,0,2:T(8,128)(4,1)} %copy.110) | copy-start | bytes 3076
  210.7 21.0 %copy-start.123 = (f32[6]{0:T(128)S(1)}, f32[6]{0:T(128)}, u32[]{:S(2)}) copy-start(f32[6]{0:T(128)} %get-tuple-element.9) | copy-start | bytes 76
  244.4 27.7 %copy-start.2 = (bf16[12,36,4,6,64]{4,3,2,1,0:T(8,128)(2,1)S(1)}, bf16[12,36,4,6,64]{4,3,2,1,0:T(8,128)(2,1)}, u32[]{:S(2)}) copy-start(bf16[12,36,4,6,64]{4,3,2,1,0:T(8,128)(2,1)} %reshape.318) | copy-start | bytes 3981316
  (117 other events, 873.2 us)
Sparse Core Ops, SparseCore 0:
  8.9 56.1 all-gather.2
  66.7 49.1 all-gather.4
  398.8 6.9 reduce-scatter.1
where the time goes:
time: 421 us; the launch traced here: 414 us
  local copies, waits for them, and re-layouts  172 us (41%)
  matrix products  154 us (37%)
  other arithmetic  41.7 us (10%)
  waiting for transfers between devices  15.8 us (4%)
  between operations  14.9 us (4%)
  starting transfers between devices  13.4 us (3%)
    dot_general x25, matrix products, local(): jnp.einsum('yxhe,yxbhe->hyxb', query_heads, window_keys, preferred_elemen...  82.2 us
    dot_general x25, matrix products, local(): jnp.einsum('hyxb,yxbhe->yxhe', share, window_values, preferred_element_ty...  64.1 us
    slice x27, local copies, waits for them, and re-layouts, local(): share = weights[..., 1 + place * BUCKET:1 + (place + 1) * BUCKET]  47.8 us
    dot_general x25, local copies, waits for them, and re-layouts, local(): jnp.einsum('yxhe,yxbhe->hyxb', query_heads, window_keys, preferred_elemen...  36.5 us
    slice x2, local copies, waits for them, and re-layouts, local(): value_heads[row_step:row_step + lat_cells, col_step:col_step + lon_cells]  32.9 us
    reduce_max x26, other arithmetic, local(): row_max = jnp.max(scores, axis=-1, keepdims=True)  27 us
    slice x2, local copies, waits for them, and re-layouts, local(): key_heads[row_step:row_step + lat_cells, col_step:col_step + lon_cells]  22 us
    slice x27, local copies, waits for them, and re-layouts, local(): filled_ext[row_step:row_step + lat_cells, col_step:col_step + lon_cells]  14.2 us
  transfers between devices with their start and end apart: 8, of which 4 were waited for; matrix products, arithmetic and copies ran while one was open for 87% of the time, Pallas kernels for 0%

commit v1 on v0

--- a/solution.py
+++ b/solution.py
@@ -1,13 +1,21 @@
+import functools
 import math
 
 import jax
 import jax.numpy as jnp
+import numpy as np
 from jax import lax
+from jax.experimental import pallas as pl
+from jax.experimental.pallas import tpu as pltpu
 from jax.sharding import PartitionSpec as P
 
 HEAD = 64
 BUCKET = 4
 REACH = 2
+SIDE = 2 * REACH + 1
+FAR = -128.0
+LOW = -1e30
+MESH = pl.DeviceIdType.MESH
 
 
 def extended(cells, sides, width):
@@ -26,7 +34,7 @@
     return cells
 
 
-def local(
+def banded(
     observations,
     send_counts,
     bucket_slots,
@@ -142,6 +150,425 @@
     return (own_rows + summed).astype(jnp.bfloat16)
 
 
+def flipped(index, step):
+    bit = 1
+    while bit <= step:
+        if step & bit:
+            index = index + bit - 2 * bit * ((index // bit) % 2)
+        bit *= 2
+    return index
+
+
+def dot_nt(a, b):
+    return lax.dot_general(a, b, (((1,), (1,)), ((), ())), preferred_element_type=jnp.float32)
+
+
+def dot_nn(a, b):
+    return jnp.dot(a, b, preferred_element_type=jnp.float32)
+
+
+def fused_kernel(
+    sizes,
+    meta_ref,
+    obs_ref,
+    spread_ref,
+    owner_ref,
+    before_ref,
+    equal_ref,
+    place_ref,
+    lat_ref,
+    gain_ref,
+    wq_ref,
+    wk_ref,
+    wv_ref,
+    head_ref,
+    wo_ref,
+    up_ref,
+    down_ref,
+    out_ref,
+    wq2_ref,
+    wk2_ref,
+    wv2_ref,
+    head2_ref,
+    wo2_ref,
+    up2_ref,
+    down2_ref,
+    tok_ref,
+    back_ref,
+    part_ref,
+    rows_ref,
+    metas_ref,
+    q_ref,
+    k_ref,
+    v_ref,
+    near_ref,
+    att_ref,
+    pair_send,
+    pair_recv,
+    tok_send,
+    tok_recv,
+    part_send,
+    part_recv,
+    obs_send,
+    obs_recv,
+    meta_send,
+    meta_recv,
+):
+    n_lat, n_lon, lat_cells, lon_cells, heads = sizes
+    half_rows = lat_cells // 2
+    tokens = half_rows * lon_cells
+    owners = n_lat * n_lon
+    group = owners * 2
+    listed = obs_ref.shape[0]
+    total = owners * listed
+    lat = lax.axis_index("lat")
+    lon = lax.axis_index("lon")
+    rep = lax.axis_index("rep")
+    owner = lat * n_lon + lon
+    me = owner * 2 + rep
+
+    def member(flat):
+        return {"lat": flat // (2 * n_lon), "lon": (flat // 2) % n_lon, "rep": flat % 2}
+
+    barrier = pltpu.get_barrier_semaphore()
+    for step in range(1, group):
+        pl.semaphore_signal(
+            barrier, inc=1, device_id=member((me + step) % group), device_id_type=MESH
+        )
+
+    x = lat_ref[pl.ds(pl.multiple_of(rep * tokens, tokens), tokens), :].astype(jnp.float32)
+    inv = lax.rsqrt(jnp.mean(x * x, axis=-1, keepdims=True) + 1e-06)
+    normed = (x * inv * gain_ref[...]).astype(jnp.bfloat16)
+    tok_ref[lat] = normed
+
+    counts = meta_ref[2:3, :]
+    first = jnp.sum(before_ref[...] * counts, axis=1, keepdims=True)
+    held = jnp.sum(equal_ref[...] * counts, axis=1, keepdims=True)
+    place = place_ref[...][:, 0:1]
+    spots = lax.broadcasted_iota(jnp.int32, (listed, obs_ref.shape[0]), 1).astype(jnp.float32)
+    pick = jnp.where((spots == first + place) & (place < held), 1.0, 0.0).astype(jnp.bfloat16)
+    packed = dot_nn(pick, obs_ref[...]).astype(jnp.bfloat16)
+    my_rows = pl.ds(pl.multiple_of(owner * listed, listed), listed)
+    rows_ref[rep, my_rows, :] = packed
+    metas_ref[owner] = meta_ref[...]
+
+    pl.semaphore_wait(barrier, group - 1)
+
+    def pair_copy(index, source, target):
+        return pltpu.make_async_remote_copy(
+            src_ref=source,
+            dst_ref=target,
+            send_sem=pair_send.at[index],
+            recv_sem=pair_recv.at[index],
+            device_id={"rep": 1 - rep},
+            device_id_type=MESH,
+        )
+
+    up_copy = pair_copy(0, up_ref, up2_ref)
+    down_copy = pair_copy(1, down_ref, down2_ref)
+    wq_copy = pair_copy(2, wq_ref, wq2_ref)
+    wk_copy = pair_copy(3, wk_ref, wk2_ref)
+    wv_copy = pair_copy(4, wv_ref, wv2_ref)
+    wo_copy = pair_copy(5, wo_ref, wo2_ref)
+    head_copy = pair_copy(6, head_ref, head2_ref)
+
+    tok_copies = []
+    for step in range(1, n_lat):
+        there = flipped(lat, step)
+        copy = pltpu.make_async_remote_copy(
+            src_ref=tok_ref.at[lat],
+            dst_ref=tok_ref.at[lat],
+            send_sem=tok_send.at[step],
+            recv_sem=tok_recv.at[step],
+            device_id={"lat": there},
+            device_id_type=MESH,
+        )
+        tok_copies.append(copy)
+        copy.start()
+    for copy in (up_copy, down_copy, wq_copy, wk_copy, wv_copy, wo_copy, head_copy):
+        copy.start()
+
+    def obs_copy(step, flat):
+        other = (me + step) % group
+        source_rows = pl.ds(pl.multiple_of((flat // 2) * listed, listed), listed)
+        return pltpu.make_async_remote_copy(
+            src_ref=rows_ref.at[flat % 2, source_rows],
+            dst_ref=rows_ref.at[flat % 2, source_rows],
+            send_sem=obs_send.at[step],
+            recv_sem=obs_recv.at[step],
+            device_id=member(other),
+            device_id_type=MESH,
+        )
+
+    def meta_copy(step, who):
+        other = (owner + step) % owners
+        return pltpu.make_async_remote_copy(
+            src_ref=metas_ref.at[who],
+            dst_ref=metas_ref.at[who],
+            send_sem=meta_send.at[step],
+            recv_sem=meta_recv.at[step],
+            device_id={"lat": other // n_lon, "lon": other % n_lon},
+            device_id_type=MESH,
+        )
+
+    for step in range(1, group):
+        obs_copy(step, me).start()
+    for step in range(1, owners):
+        meta_copy(step, owner).start()
+
+    halves = ((up_ref, down_ref), (up2_ref, down2_ref))
+
+    def fed(value):
+        result = None
+        for up, down in halves:
+            hidden = jax.nn.gelu(dot_nt(value, up[...]), approximate=True).astype(jnp.bfloat16)
+            term = dot_nn(hidden, down[...])
+            result = term if result is None else result + term
+        return result
+
+    up_copy.wait_recv()
+    down_copy.wait_recv()
+    part_copies = []
+    for step in range(1, n_lat):
+        there = flipped(lat, step)
+        tok_copies[step - 1].wait_recv()
+        back_ref[step] = fed(tok_ref[there]).astype(jnp.bfloat16)
+        copy = pltpu.make_async_remote_copy(
+            src_ref=back_ref.at[step],
+            dst_ref=part_ref.at[step],
+            send_sem=part_send.at[step],
+            recv_sem=part_recv.at[step],
+            device_id={"lat": there},
+            device_id_type=MESH,
+        )
+        part_copies.append(copy)
+        copy.start()
+
+    att_ref[...] = x + fed(normed)
+
+    for step in range(1, group):
+        obs_copy(step, (me + group - step) % group).wait_recv()
+    for step in range(1, owners):
+        meta_copy(step, (owner + owners - step) % owners).wait_recv()
+
+    spread = spread_ref[...]
+    own_lane = owner_ref[...]
+    y_all = metas_ref[:, 0, :].astype(jnp.bfloat16)
+    x_all = metas_ref[:, 1, :].astype(jnp.bfloat16)
+    key_y = jnp.sum(dot_nn(y_all, spread) * own_lane, axis=0, keepdims=True)
+    key_x = jnp.sum(dot_nn(x_all, spread) * own_lane, axis=0, keepdims=True)
+    query_x = (
+        lax.broadcasted_iota(jnp.int32, (lon_cells, total), 0) + lon * lon_cells
+    ).astype(jnp.float32)
+    wide = float(n_lon * lon_cells)
+    off_x = key_x - query_x + float(REACH)
+    off_x = jnp.where(off_x < 0, off_x + wide, off_x)
+    near_ref[...] = jnp.where(off_x >= wide, off_x - wide, off_x)
+    query_y = (
+        lax.broadcasted_iota(jnp.int32, (half_rows, total), 0)
+        + (lat * lat_cells + rep * half_rows)
+    ).astype(jnp.float32)
+    off_y = key_y - query_y + float(REACH)
+
+    widened = jnp.concatenate([rows_ref[0], rows_ref[1]], axis=1)
+    wq_copy.wait_recv()
+    wk_copy.wait_recv()
+    wv_copy.wait_recv()
+    wo_copy.wait_recv()
+    head_copy.wait_recv()
+    scale = 1.0 / math.sqrt(HEAD)
+
+    for wq, wk, wv, wo, per_head in (
+        (wq_ref, wk_ref, wv_ref, wo_ref, head_ref),
+        (wq2_ref, wk2_ref, wv2_ref, wo2_ref, head2_ref),
+    ):
+        queries = (dot_nn(normed, wq[...]).astype(jnp.bfloat16) * scale).astype(jnp.bfloat16)
+        keys = dot_nn(widened, wk[...]).astype(jnp.bfloat16)
+        values = dot_nn(widened, wv[...]).astype(jnp.bfloat16)
+        for h in range(heads):
+            lanes = slice(h * HEAD, (h + 1) * HEAD)
+            q_ref[h] = queries[:, lanes]
+            k_ref[h] = keys[:, lanes]
+            v_ref[h] = values[:, lanes]
+
+        def one_head(h, carry):
+            q = q_ref[h]
+            info = per_head[h]
+            null_key = info[0:1, :HEAD]
+            null_value = info[1:2, :HEAD]
+            scores = dot_nt(q, k_ref[h])
+            null_score = jnp.sum(q.astype(jnp.float32) * null_key, axis=1, keepdims=True)
+            shifts = []
+            for q_step in range(SIDE):
+                shift = jnp.full(off_y.shape, LOW, jnp.float32)
+                for p_step in range(SIDE):
+                    at = p_step * SIDE + q_step
+                    shift = jnp.where(off_y == float(p_step), info[2:3, at : at + 1], shift)
+                shifts.append(shift)
+            near = near_ref[...]
+            biases = []
+            for row in range(half_rows):
+                bias = jnp.full(near.shape, LOW, jnp.float32)
+                for q_step in range(SIDE):
+                    bias = jnp.where(
+                        near == float(q_step), shifts[q_step][row : row + 1, :], bias
+                    )
+                biases.append(bias)
+            scores = scores + jnp.concatenate(biases, axis=0)
+            top = jnp.maximum(jnp.max(scores, axis=1, keepdims=True), null_score)
+            grown = jnp.exp(scores - top)
+            null_grown = jnp.exp(null_score - top)
+            share = 1.0 / (jnp.sum(grown, axis=1, keepdims=True) + null_grown)
+            weights = (grown * share).astype(jnp.bfloat16)
+            null_weight = (null_grown * share).astype(jnp.bfloat16).astype(jnp.float32)
+            mixed = (dot_nn(weights, v_ref[h]) + null_weight * null_value).astype(jnp.bfloat16)
+            rows = pl.ds(pl.multiple_of(h * HEAD, HEAD), HEAD)
+            att_ref[...] += dot_nn(mixed, wo[rows, :])
+            return carry
+
+        lax.fori_loop(0, heads, one_head, 0)
+
+    result = att_ref[...]
+    for step in range(1, n_lat):
+        part_copies[step - 1].wait_recv()
+        result = result + part_ref[step].astype(jnp.float32)
+    out_ref[...] = result.astype(jnp.bfloat16)
+
+    for copy in tok_copies + part_copies:
+        copy.wait_send()
+    for copy in (up_copy, down_copy, wq_copy, wk_copy, wv_copy, wo_copy, head_copy):
+        copy.wait_send()
+    for step in range(1, group):
+        obs_copy(step, me).wait_send()
+    for step in range(1, owners):
+        meta_copy(step, owner).wait_send()
+
+
+def fused(
+    n_lat,
+    n_lon,
+    observations,
+    send_counts,
+    bucket_slots,
+    latent,
+    norm_gain,
+    w_query,
+    w_key,
+    w_value,
+    null_kv,
+    rel_bias,
+    w_out,
+    w_up,
+    w_down,
+):
+    lat_cells, lon_cells, depth = latent.shape
+    owners = n_lat * n_lon
+    cap = bucket_slots.shape[2]
+    listed = observations.shape[0]
+    total = owners * listed
+    half_chan = observations.shape[1]
+    heads = w_query.shape[1] // HEAD
+    tokens = lat_cells * lon_cells // 2
+    lanes = 128
+
+    slots = bucket_slots[0].reshape(-1)
+    row_slots = lon_cells * BUCKET
+    valid = slots < lat_cells * row_slots
+    cell_y = lax.axis_index("lat") * lat_cells + slots // row_slots
+    cell_x = lax.axis_index("lon") * lon_cells + (slots // BUCKET) % lon_cells
+    y_line = jnp.where(valid, cell_y.astype(jnp.float32), FAR)
+    x_line = jnp.where(valid, cell_x.astype(jnp.float32), 0.0)
+    count_line = send_counts[0].astype(jnp.float32)
+    meta = jnp.zeros((8, lanes), jnp.float32)
+    meta = jnp.concatenate(
+        [
+            jnp.pad(line, (0, lanes - line.shape[0]))[None]
+            for line in (y_line, x_line, count_line)
+        ]
+        + [jnp.zeros((5, lanes), jnp.float32)],
+        axis=0,
+    )
+    nulls = jnp.transpose(null_kv.astype(jnp.float32).reshape(2, heads, HEAD), (1, 0, 2))
+    per_head = jnp.concatenate(
+        [
+            jnp.pad(nulls, ((0, 0), (0, 0), (0, lanes - HEAD))),
+            jnp.pad(rel_bias, ((0, 0), (0, lanes - rel_bias.shape[1])))[:, None],
+            jnp.zeros((heads, 5, lanes), jnp.float32),
+        ],
+        axis=1,
+    )
+
+    lane = np.arange(total)
+    line = np.arange(lanes)
+    entry = np.arange(listed)
+    spread = line[:, None] == ((lane // (owners * cap)) * cap + lane % cap)[None]
+    own_lane = np.arange(owners)[:, None] == ((lane // cap) % owners)[None]
+    before = line[None] < (entry // cap)[:, None]
+    equal = line[None] == (entry // cap)[:, None]
+    places = np.broadcast_to((entry % cap)[:, None], (listed, lanes))
+
+    bf16 = jnp.bfloat16
+    args = (
+        meta,
+        observations,
+        jnp.asarray(spread, bf16),
+        jnp.asarray(own_lane, jnp.float32),
+        jnp.asarray(before, jnp.float32),
+        jnp.asarray(equal, jnp.float32),
+        jnp.asarray(places, jnp.float32),
+        latent.reshape(lat_cells * lon_cells, depth),
+        norm_gain.reshape(1, depth),
+        w_query,
+        w_key,
+        w_value,
+        per_head,
+        w_out,
+        w_up,
+        w_down,
+    )
+    dma = pltpu.SemaphoreType.DMA
+    group = 2 * owners
+    out = pl.pallas_call(
+        functools.partial(fused_kernel, (n_lat, n_lon, lat_cells, lon_cells, heads)),
+        out_shape=jax.ShapeDtypeStruct((tokens, depth), bf16),
+        in_specs=[pl.BlockSpec(memory_space=pltpu.VMEM)] * len(args),
+        out_specs=pl.BlockSpec(memory_space=pltpu.VMEM),
+        scratch_shapes=[
+            pltpu.VMEM(w_query.shape, bf16),
+            pltpu.VMEM(w_key.shape, bf16),
+            pltpu.VMEM(w_value.shape, bf16),
+            pltpu.VMEM(per_head.shape, jnp.float32),
+            pltpu.VMEM(w_out.shape, bf16),
+            pltpu.VMEM(w_up.shape, bf16),
+            pltpu.VMEM(w_down.shape, bf16),
+            pltpu.VMEM((n_lat, tokens, depth), bf16),
+            pltpu.VMEM((n_lat, tokens, depth), bf16),
+            pltpu.VMEM((n_lat, tokens, depth), bf16),
+            pltpu.VMEM((2, total, half_chan), bf16),
+            pltpu.VMEM((owners,) + meta.shape, jnp.float32),
+            pltpu.VMEM((heads, tokens, HEAD), bf16),
+            pltpu.VMEM((heads, total, HEAD), bf16),
+            pltpu.VMEM((heads, total, HEAD), bf16),
+            pltpu.VMEM((lon_cells, total), jnp.float32),
+            pltpu.VMEM((tokens, depth), jnp.float32),
+            dma((7,)),
+            dma((7,)),
+            dma((n_lat,)),
+            dma((n_lat,)),
+            dma((n_lat,)),
+            dma((n_lat,)),
+            dma((group,)),
+            dma((group,)),
+            dma((owners,)),
+            dma((owners,)),
+        ],
+        compiler_params=pltpu.CompilerParams(
+            collective_id=0, has_side_effects=True, vmem_limit_bytes=48 * 2**20
+        ),
+    )(*args)
+    return out.reshape(lat_cells // 2, lon_cells, depth)
+
+
 def solution(mesh):
     in_specs = (
         P(("parts", "lat", "lon"), "rep"),
@@ -159,4 +586,18 @@
         P(("lat", "rep"), None),
     )
     out_specs = P(("parts", "lat", "rep"), "lon", None)
+    n_lat, n_lon, n_rep = mesh.shape["lat"], mesh.shape["lon"], mesh.shape["rep"]
+
+    def local(observations, send_counts, bucket_slots, *rest):
+        cap = bucket_slots.shape[2]
+        listed = n_lat * n_lon * cap
+        direct = (
+            n_rep == 2
+            and n_lat in (2, 4)
+            and listed <= 128
+            and observations.shape[0] == listed
+        )
+        step = functools.partial(fused, n_lat, n_lon) if direct else banded
+        return step(observations, send_counts, bucket_slots, *rest)
+
     return jax.shard_map(local, mesh=mesh, in_specs=in_specs, out_specs=out_specs, check_vma=False)

time: 421 us -> 67.7 us (0.16); the launches traced: 414 us -> 66.9 us
  local copies, waits for them, and re-layouts: 172 us -> 14.5 us
  matrix products: 154 us -> 0 us
  Pallas kernels: 0 us -> 51.5 us
  other arithmetic: 41.7 us -> 0.87 us
  waiting for transfers between devices: 15.8 us -> 0 us
  between operations: 14.9 us -> 0.05 us
  starting transfers between devices: 13.4 us -> 0 us
    dot_general x56 -> x0, matrix products: 154 us -> none  [the longest x25 82.2 us: local(): jnp.einsum('yxhe,yxbhe->hyxb', query_heads, window_keys, preferred_elemen...]
    slice x66 -> x0, local copies, waits for them, and re-layouts: 119 us -> none  [the longest x27 47.8 us: local(): share = weights[..., 1 + place * BUCKET:1 + (place + 1) * BUCKET]]
    pallas_call x0 -> x1, Pallas kernels: none -> 51.5 us  [fused(): pl.pallas_call(functools.partial(fused_kernel, (n_lat, n_lon, lat_cells,...]
    dot_general x26 -> x0, local copies, waits for them, and re-layouts: 36.6 us -> none  [the longest x25 36.5 us: local(): jnp.einsum('yxhe,yxbhe->hyxb', query_heads, window_keys, preferred_elemen...]
    reduce_max x26 -> x0, other arithmetic: 27 us -> none  [local(): row_max = jnp.max(scores, axis=-1, keepdims=True)]
    unnamed x268 -> x27, local copies, waits for them, and re-layouts: 2.32 us -> 11.5 us
    reshape x6 -> x3, local copies, waits for them, and re-layouts: 9.38 us -> 1.46 us  [the longest x2 0.77 us: fused(): null_kv.astype(jnp.float32).reshape(2, heads, HEAD)]
    ppermute x4 -> x0, waiting for transfers between devices: 7.27 us -> none  [the longest x2 4.19 us: extended(): lax.ppermute(tail, axis, [(i, (i + 1) % count) for i in range(count)])]
  transfers between devices with their start and end apart: 8 -> 0, of which waited for: 4 -> 0; matrix products, arithmetic and copies ran while one was open for 87% -> 0% of each run, Pallas kernels for 0% -> 0%
where the time goes in v1:
time: 67.7 us; the launch traced here: 66.9 us
  Pallas kernels  51.5 us (76%)
  local copies, waits for them, and re-layouts  14.5 us (21%)
  other arithmetic  0.87 us (1%)
    pallas_call x1, Pallas kernels, fused(): pl.pallas_call(functools.partial(fused_kernel, (n_lat, n_lon, lat_cells,...  51.5 us
    unnamed x27, local copies, waits for them, and re-layouts  11.5 us

profile of v1, /device:TPU:0, one launch (start us, length us, event | category | flops | bytes accessed | tf_op | source)
XLA Modules:
  0.0 66.9 jit_solution(14755778605432230608)
XLA Ops:
  0.0 0.0 copy-start.7
  0.0 0.7 %convert_bitcast_fusion = f32[8]{0:T(128)S(1)} fusion(s32[1,8]{1,0:T(1,128)} %param.19), kind=kLoop, calls=%fused_computation.20 | loop fusion | flops 8 | bytes 64 | tf_op jit(solution)/shard_map/convert_element_type | solution.py:481
  0.7 0.8 %reshape_squeeze.3 = s32[64]{0:T(128)S(1)} reshape(s32[1,8,8]{2,1,0:T(8,128)} %param.20) | data formatting | bytes 512 | tf_op jit(solution)/shard_map/reshape;squeeze | solution.py:474
  1.5 0.1 pad.34.clone
  1.6 0.1 maximum_maximum_fusion.1.meta_ref
  1.7 0.7 %reshape.15.gain_ref = f32[1,768]{1,0:T(1,128)S(1)} reshape(f32[768]{0:T(1024)} %param.22) | data formatting | bytes 6144 | tf_op jit(solution)/shard_map/reshape | solution.py:520
  2.4 0.8 %reshape.16 = bf16[2,6,64]{2,1,0:T(8,128)(2,1)S(1)} reshape(bf16[2,384]{1,0:T(2,128)(2,1)} %param.26) | data formatting | bytes 3072 | tf_op jit(solution)/shard_map/reshape | solution.py:491
  3.1 0.7 %pad.27 = f32[6,128]{1,0:T(8,128)S(1)} pad(f32[6,25]{1,0:T(8,128)} %param.27, f32[]{:T(128)} %constant.67.clone.1), padding=0_0x0_103 | pad | bytes 3676 | tf_op jit(solution)/shard_map/jit(_pad)/pad | solution.py:495
  3.8 0.1 maximum_maximum_fusion.head_ref
  3.9 0.0 copy-done.7
  3.9 1.1 %copy-done = bf16[768,384]{1,0:T(8,128)(2,1)S(1)} copy-done((bf16[768,384]{1,0:T(8,128)(2,1)S(1)}, bf16[768,384]{1,0:T(8,128)(2,1)}, u32[]{:S(2)}) %copy-start) | copy-done | bytes 589848
  5.0 1.1 %copy-done.1 = bf16[384,768]{1,0:T(8,128)(2,1)S(1)} copy-done((bf16[384,768]{1,0:T(8,128)(2,1)S(1)}, bf16[384,768]{1,0:T(8,128)(2,1)}, u32[]{:S(2)}) %copy-start.1) | copy-done | bytes 589848
  6.0 1.1 %copy-done.2 = bf16[384,768]{1,0:T(8,128)(2,1)S(1)} copy-done((bf16[384,768]{1,0:T(8,128)(2,1)S(1)}, bf16[384,768]{1,0:T(8,128)(2,1)}, u32[]{:S(2)}) %copy-start.2) | copy-done | bytes 589848
  7.1 1.1 %copy-done.3 = bf16[384,768]{1,0:T(8,128)(2,1)S(1)} copy-done((bf16[384,768]{1,0:T(8,128)(2,1)S(1)}, bf16[384,768]{1,0:T(8,128)(2,1)}, u32[]{:S(2)}) %copy-start.3) | copy-done | bytes 589848
  8.2 1.0 %copy-done.4 = bf16[8,32,768]{2,1,0:T(8,128)(2,1)S(1)} copy-done((bf16[8,32,768]{2,1,0:T(8,128)(2,1)S(1)}, bf16[8,32,768]{2,1,0:T(8,128)(2,1)}, u32[]{:S(2)}) %copy-start.4) | copy-done | bytes 393240
  9.2 0.9 %copy-done.5 = bf16[256,384]{1,0:T(8,128)(2,1)S(1)} copy-done((bf16[256,384]{1,0:T(8,128)(2,1)S(1)}, bf16[256,384]{1,0:T(8,128)(2,1)}, u32[]{:S(2)}) %copy-start.5) | copy-done | bytes 196632
  10.1 0.9 %copy-done.6 = bf16[256,384]{1,0:T(8,128)(2,1)S(1)} copy-done((bf16[256,384]{1,0:T(8,128)(2,1)S(1)}, bf16[256,384]{1,0:T(8,128)(2,1)}, u32[]{:S(2)}) %copy-start.6) | copy-done | bytes 196632
  11.0 0.8 %copy-done.8 = f32[64,128]{1,0:T(8,128)S(1)} copy-done((f32[64,128]{1,0:T(8,128)S(1)}, f32[64,128]{1,0:T(8,128)}, u32[]{:S(2)}) %copy-start.8) | copy-done | bytes 32792
  11.8 0.8 %copy-done.9 = f32[64,128]{1,0:T(8,128)S(1)} copy-done((f32[64,128]{1,0:T(8,128)S(1)}, f32[64,128]{1,0:T(8,128)}, u32[]{:S(2)}) %copy-start.9) | copy-done | bytes 32792
  12.5 0.8 %copy-done.10 = f32[64,128]{1,0:T(8,128)S(1)} copy-done((f32[64,128]{1,0:T(8,128)S(1)}, f32[64,128]{1,0:T(8,128)}, u32[]{:S(2)}) %copy-start.10) | copy-done | bytes 32792
  13.3 0.7 %copy-done.11 = bf16[64,128]{1,0:T(8,128)(2,1)S(1)} copy-done((bf16[64,128]{1,0:T(8,128)(2,1)S(1)}, bf16[64,128]{1,0:T(8,128)(2,1)}, u32[]{:S(2)}) %copy-start.11) | copy-done | bytes 16408
  14.0 0.7 %copy-done.12 = f32[8,512]{1,0:T(8,128)S(1)} copy-done((f32[8,512]{1,0:T(8,128)S(1)}, f32[8,512]{1,0:T(8,128)}, u32[]{:S(2)}) %copy-start.12) | copy-done | bytes 16408
  14.7 51.5 %shard_map.172 = bf16[128,768]{1,0:T(8,128)(2,1)S(1)} custom-call(f32[8,128]{1,0:T(8,128)S(1)} %maximum_maximum_fusion.1.meta_ref, bf16[64,128]{1,0:T(8,128)(2,1)S(1)} %copy-done.11, bf16[128,512]{1,0:T(8,128)(2,1)S(1)} %copy-done.7, f32[8,512]{1,0:T(8,128)S(1)} %copy-done.12, f32[64,128]{1,0:T(8,128)S(1)} %copy-done.10, f32[64,128]{1,0:T(8,128)S(1)} %copy-done.9, ...), custom_call_target="tpu_custom_call" | custom-call | tf_op jit(solution)/shard_map/pallas_call | solution.py:531
  66.2 0.7 %copy.23 = bf16[4,32,768]{2,1,0:T(8,128)(2,1)} copy(bf16[4,32,768]{2,1,0:T(8,128)(2,1)S(1)} %bitcast.13) | data formatting | bytes 393216
  (19 shorter events, 0.1 us)
Async XLA Ops:
  0.0 3.9 %copy-start.7 = (bf16[128,512]{1,0:T(8,128)(2,1)S(1)}, bf16[128,512]{1,0:T(8,128)(2,1)}, u32[]{:S(2)}) copy-start(bf16[128,512]{1,0:T(8,128)(2,1)} %constant.74.clone.spread_ref) | copy-start | bytes 393220
  3.9 1.1 %copy-start = (bf16[768,384]{1,0:T(8,128)(2,1)S(1)}, bf16[768,384]{1,0:T(8,128)(2,1)}, u32[]{:S(2)}) copy-start(bf16[768,384]{1,0:T(8,128)(2,1)} %wq_ref.1) | copy-start | bytes 1769476
  5.0 1.1 %copy-start.1 = (bf16[384,768]{1,0:T(8,128)(2,1)S(1)}, bf16[384,768]{1,0:T(8,128)(2,1)}, u32[]{:S(2)}) copy-start(bf16[384,768]{1,0:T(8,128)(2,1)} %wo_ref.1) | copy-start | bytes 1769476
  6.0 1.1 %copy-start.2 = (bf16[384,768]{1,0:T(8,128)(2,1)S(1)}, bf16[384,768]{1,0:T(8,128)(2,1)}, u32[]{:S(2)}) copy-start(bf16[384,768]{1,0:T(8,128)(2,1)} %up_ref.1) | copy-start | bytes 1769476
  7.1 1.1 %copy-start.3 = (bf16[384,768]{1,0:T(8,128)(2,1)S(1)}, bf16[384,768]{1,0:T(8,128)(2,1)}, u32[]{:S(2)}) copy-start(bf16[384,768]{1,0:T(8,128)(2,1)} %down_ref.1) | copy-start | bytes 1769476
  8.2 1.0 %copy-start.4 = (bf16[8,32,768]{2,1,0:T(8,128)(2,1)S(1)}, bf16[8,32,768]{2,1,0:T(8,128)(2,1)}, u32[]{:S(2)}) copy-start(bf16[8,32,768]{2,1,0:T(8,128)(2,1)} %param.21) | copy-start | bytes 1179652
  9.2 0.9 %copy-start.5 = (bf16[256,384]{1,0:T(8,128)(2,1)S(1)}, bf16[256,384]{1,0:T(8,128)(2,1)}, u32[]{:S(2)}) copy-start(bf16[256,384]{1,0:T(8,128)(2,1)} %wk_ref.1) | copy-start | bytes 589828
  10.1 0.9 %copy-start.6 = (bf16[256,384]{1,0:T(8,128)(2,1)S(1)}, bf16[256,384]{1,0:T(8,128)(2,1)}, u32[]{:S(2)}) copy-start(bf16[256,384]{1,0:T(8,128)(2,1)} %wv_ref.1) | copy-start | bytes 589828
  11.0 0.8 %copy-start.8 = (f32[64,128]{1,0:T(8,128)S(1)}, f32[64,128]{1,0:T(8,128)}, u32[]{:S(2)}) copy-start(f32[64,128]{1,0:T(8,128)} %constant.78.clone.place_ref) | copy-start | bytes 98308
  11.8 0.8 %copy-start.9 = (f32[64,128]{1,0:T(8,128)S(1)}, f32[64,128]{1,0:T(8,128)}, u32[]{:S(2)}) copy-start(f32[64,128]{1,0:T(8,128)} %constant.77.clone.equal_ref) | copy-start | bytes 98308
  12.5 0.8 %copy-start.10 = (f32[64,128]{1,0:T(8,128)S(1)}, f32[64,128]{1,0:T(8,128)}, u32[]{:S(2)}) copy-start(f32[64,128]{1,0:T(8,128)} %constant.76.clone.before_ref) | copy-start | bytes 98308
  13.3 0.7 %copy-start.11 = (bf16[64,128]{1,0:T(8,128)(2,1)S(1)}, bf16[64,128]{1,0:T(8,128)(2,1)}, u32[]{:S(2)}) copy-start(bf16[64,128]{1,0:T(8,128)(2,1)} %obs_ref.1) | copy-start | bytes 49156
  14.0 0.7 %copy-start.12 = (f32[8,512]{1,0:T(8,128)S(1)}, f32[8,512]{1,0:T(8,128)}, u32[]{:S(2)}) copy-start(f32[8,512]{1,0:T(8,128)} %constant.75.clone.owner_ref) | copy-start | bytes 49156

commit v2 on v1

--- a/solution.py
+++ b/solution.py
@@ -3,7 +3,6 @@
 
 import jax
 import jax.numpy as jnp
-import numpy as np
 from jax import lax
 from jax.experimental import pallas as pl
 from jax.experimental.pallas import tpu as pltpu
@@ -150,15 +149,6 @@
     return (own_rows + summed).astype(jnp.bfloat16)
 
 
-def flipped(index, step):
-    bit = 1
-    while bit <= step:
-        if step & bit:
-            index = index + bit - 2 * bit * ((index // bit) % 2)
-        bit *= 2
-    return index
-
-
 def dot_nt(a, b):
     return lax.dot_general(a, b, (((1,), (1,)), ((), ())), preferred_element_type=jnp.float32)
 
@@ -169,32 +159,43 @@
 
 def fused_kernel(
     sizes,
-    meta_ref,
+    obs_hbm,
+    counts_hbm,
+    slots_hbm,
+    lat_hbm,
+    gain_hbm,
+    wq_hbm,
+    wk_hbm,
+    wv_hbm,
+    null_ref,
+    bias_hbm,
+    wo_hbm,
+    up_hbm,
+    down_hbm,
+    out_ref,
     obs_ref,
-    spread_ref,
-    owner_ref,
-    before_ref,
-    equal_ref,
-    place_ref,
+    counts_ref,
+    slots_ref,
     lat_ref,
     gain_ref,
     wq_ref,
     wk_ref,
     wv_ref,
-    head_ref,
+    bias_ref,
     wo_ref,
     up_ref,
     down_ref,
-    out_ref,
     wq2_ref,
     wk2_ref,
     wv2_ref,
+    head_ref,
     head2_ref,
     wo2_ref,
     up2_ref,
     down2_ref,
     tok_ref,
     back_ref,
+    send_ref,
     part_ref,
     rows_ref,
     metas_ref,
@@ -203,6 +204,7 @@
     v_ref,
     near_ref,
     att_ref,
+    load_sem,
     pair_send,
     pair_recv,
     tok_send,
@@ -219,8 +221,10 @@
     tokens = half_rows * lon_cells
     owners = n_lat * n_lon
     group = owners * 2
-    listed = obs_ref.shape[0]
+    cap = slots_ref.shape[2]
+    listed = owners * cap
     total = owners * listed
+    hops = n_lat - 1
     lat = lax.axis_index("lat")
     lon = lax.axis_index("lon")
     rep = lax.axis_index("rep")
@@ -236,21 +240,61 @@
             barrier, inc=1, device_id=member((me + step) % group), device_id_type=MESH
         )
 
-    x = lat_ref[pl.ds(pl.multiple_of(rep * tokens, tokens), tokens), :].astype(jnp.float32)
+    half = pl.ds(rep * half_rows, half_rows)
+    loads = [
+        pltpu.make_async_copy(source, target, load_sem.at[index])
+        for index, (source, target) in enumerate(
+            (
+                (lat_hbm.at[half], lat_ref),
+                (gain_hbm, gain_ref),
+                (obs_hbm, obs_ref),
+                (counts_hbm, counts_ref),
+                (slots_hbm, slots_ref),
+                (bias_hbm, bias_ref),
+                (up_hbm, up_ref),
+                (down_hbm, down_ref),
+                (wq_hbm, wq_ref),
+                (wk_hbm, wk_ref),
+                (wv_hbm, wv_ref),
+                (wo_hbm, wo_ref),
+            )
+        )
+    ]
+    for load in loads:
+        load.start()
+    for load in loads[:6]:
+        load.wait()
+
+    x = lat_ref[...].astype(jnp.float32).reshape(tokens, lat_ref.shape[2])
     inv = lax.rsqrt(jnp.mean(x * x, axis=-1, keepdims=True) + 1e-06)
     normed = (x * inv * gain_ref[...]).astype(jnp.bfloat16)
     tok_ref[lat] = normed
-
-    counts = meta_ref[2:3, :]
-    first = jnp.sum(before_ref[...] * counts, axis=1, keepdims=True)
-    held = jnp.sum(equal_ref[...] * counts, axis=1, keepdims=True)
-    place = place_ref[...][:, 0:1]
-    spots = lax.broadcasted_iota(jnp.int32, (listed, obs_ref.shape[0]), 1).astype(jnp.float32)
+    att_ref[...] = x
+
+    entry = lax.broadcasted_iota(jnp.int32, (listed, owners), 0)
+    column = lax.broadcasted_iota(jnp.int32, (listed, owners), 1)
+    counts = counts_ref[...]
+    first = jnp.sum(jnp.where(column < entry // cap, counts, 0), axis=1, keepdims=True)
+    held = jnp.sum(jnp.where(column == entry // cap, counts, 0), axis=1, keepdims=True)
+    place = entry[:, 0:1] % cap
+    spots = lax.broadcasted_iota(jnp.int32, (listed, obs_ref.shape[0]), 1)
     pick = jnp.where((spots == first + place) & (place < held), 1.0, 0.0).astype(jnp.bfloat16)
-    packed = dot_nn(pick, obs_ref[...]).astype(jnp.bfloat16)
     my_rows = pl.ds(pl.multiple_of(owner * listed, listed), listed)
-    rows_ref[rep, my_rows, :] = packed
-    metas_ref[owner] = meta_ref[...]
+    rows_ref[rep, my_rows, :] = dot_nn(pick, obs_ref[...]).astype(jnp.bfloat16)
+
+    slots = slots_ref[0]
+    row_slots = lon_cells * BUCKET
+    cell_y = (lat * lat_cells + slots // row_slots).astype(jnp.float32)
+    cell_x = (lon * lon_cells + (slots // BUCKET) % lon_cells).astype(jnp.float32)
+    metas_ref[owner] = jnp.zeros(metas_ref.shape[1:], jnp.float32)
+    metas_ref[owner, 0, :, 0:cap] = jnp.where(slots < lat_cells * row_slots, cell_y, FAR)
+    metas_ref[owner, 1, :, 0:cap] = cell_x
+
+    nulls = null_ref[...].astype(jnp.float32)
+    head_ref[...] = jnp.zeros(head_ref.shape, jnp.float32)
+    for h in range(heads):
+        head_ref[h, 0:2, 0:HEAD] = nulls[:, h * HEAD : (h + 1) * HEAD]
+        head_ref[h, 2:3, 0 : SIDE * SIDE] = bias_ref[h : h + 1, :]
 
     pl.semaphore_wait(barrier, group - 1)
 
@@ -264,39 +308,48 @@
             device_id_type=MESH,
         )
 
-    up_copy = pair_copy(0, up_ref, up2_ref)
-    down_copy = pair_copy(1, down_ref, down2_ref)
-    wq_copy = pair_copy(2, wq_ref, wq2_ref)
-    wk_copy = pair_copy(3, wk_ref, wk2_ref)
-    wv_copy = pair_copy(4, wv_ref, wv2_ref)
-    wo_copy = pair_copy(5, wo_ref, wo2_ref)
+    up_copy = pair_copy(0, up_hbm, up2_ref)
+    down_copy = pair_copy(1, down_hbm, down2_ref)
+    wq_copy = pair_copy(2, wq_hbm, wq2_ref)
+    wk_copy = pair_copy(3, wk_hbm, wk2_ref)
+    wv_copy = pair_copy(4, wv_hbm, wv2_ref)
+    wo_copy = pair_copy(5, wo_hbm, wo2_ref)
     head_copy = pair_copy(6, head_ref, head2_ref)
 
-    tok_copies = []
-    for step in range(1, n_lat):
-        there = flipped(lat, step)
-        copy = pltpu.make_async_remote_copy(
-            src_ref=tok_ref.at[lat],
-            dst_ref=tok_ref.at[lat],
-            send_sem=tok_send.at[step],
-            recv_sem=tok_recv.at[step],
-            device_id={"lat": there},
+    def within(index):
+        return (index >= 0) & (index < n_lat)
+
+    def tok_copy(way, hop, source):
+        at = (way > 0) * hops + hop
+        return pltpu.make_async_remote_copy(
+            src_ref=tok_ref.at[source],
+            dst_ref=tok_ref.at[source],
+            send_sem=tok_send.at[at],
+            recv_sem=tok_recv.at[at],
+            device_id={"lat": lat + way},
             device_id_type=MESH,
         )
-        tok_copies.append(copy)
-        copy.start()
-    for copy in (up_copy, down_copy, wq_copy, wk_copy, wv_copy, wo_copy, head_copy):
-        copy.start()
-
-    def obs_copy(step, flat):
-        other = (me + step) % group
-        source_rows = pl.ds(pl.multiple_of((flat // 2) * listed, listed), listed)
+
+    def sum_copy(way, hop):
+        at = (way > 0) * hops + hop
         return pltpu.make_async_remote_copy(
-            src_ref=rows_ref.at[flat % 2, source_rows],
-            dst_ref=rows_ref.at[flat % 2, source_rows],
+            src_ref=send_ref.at[at],
+            dst_ref=part_ref.at[at],
+            send_sem=part_send.at[at],
+            recv_sem=part_recv.at[at],
+            device_id={"lat": lat - way},
+            device_id_type=MESH,
+        )
+
+    def obs_copy(step, who):
+        other = (owner + step) % owners
+        source_rows = pl.ds(pl.multiple_of(who * listed, listed), listed)
+        return pltpu.make_async_remote_copy(
+            src_ref=rows_ref.at[rep, source_rows],
+            dst_ref=rows_ref.at[rep, source_rows],
             send_sem=obs_send.at[step],
             recv_sem=obs_recv.at[step],
-            device_id=member(other),
+            device_id={"lat": other // n_lon, "lon": other % n_lon},
             device_id_type=MESH,
         )
 
@@ -311,10 +364,21 @@
             device_id_type=MESH,
         )
 
-    for step in range(1, group):
-        obs_copy(step, me).start()
+    ways = (1, -1)
+    for way in ways:
+
+        @pl.when(within(lat + way))
+        def _():
+            tok_copy(way, 0, lat).start()
+
+    pair_copies = (up_copy, down_copy, wq_copy, wk_copy, wv_copy, wo_copy, head_copy)
+    for copy in pair_copies:
+        copy.start()
     for step in range(1, owners):
+        obs_copy(step, owner).start()
         meta_copy(step, owner).start()
+    rows_copy = pair_copy(7, rows_ref.at[rep], rows_ref.at[rep])
+    back_rows = pair_copy(7, rows_ref.at[1 - rep], rows_ref.at[1 - rep])
 
     halves = ((up_ref, down_ref), (up2_ref, down2_ref))
 
@@ -328,35 +392,29 @@
 
     up_copy.wait_recv()
     down_copy.wait_recv()
-    part_copies = []
-    for step in range(1, n_lat):
-        there = flipped(lat, step)
-        tok_copies[step - 1].wait_recv()
-        back_ref[step] = fed(tok_ref[there]).astype(jnp.bfloat16)
-        copy = pltpu.make_async_remote_copy(
-            src_ref=back_ref.at[step],
-            dst_ref=part_ref.at[step],
-            send_sem=part_send.at[step],
-            recv_sem=part_recv.at[step],
-            device_id={"lat": there},
-            device_id_type=MESH,
-        )
-        part_copies.append(copy)
-        copy.start()
-
-    att_ref[...] = x + fed(normed)
-
-    for step in range(1, group):
-        obs_copy(step, (me + group - step) % group).wait_recv()
+    for load in loads[6:]:
+        load.wait()
+
+    for step in range(1, owners):
+        obs_copy(step, (owner + owners - step) % owners).wait_recv()
+    rows_copy.start()
     for step in range(1, owners):
         meta_copy(step, (owner + owners - step) % owners).wait_recv()
 
-    spread = spread_ref[...]
-    own_lane = owner_ref[...]
-    y_all = metas_ref[:, 0, :].astype(jnp.bfloat16)
-    x_all = metas_ref[:, 1, :].astype(jnp.bfloat16)
-    key_y = jnp.sum(dot_nn(y_all, spread) * own_lane, axis=0, keepdims=True)
-    key_x = jnp.sum(dot_nn(x_all, spread) * own_lane, axis=0, keepdims=True)
+    lane = lax.broadcasted_iota(jnp.int32, (128, total), 1)
+    line = lax.broadcasted_iota(jnp.int32, (128, total), 0)
+    spread = jnp.where(lane % cap == line, 1.0, 0.0).astype(jnp.bfloat16)
+    pair_lane = lax.broadcasted_iota(jnp.int32, (listed, total), 1)
+    pair_line = lax.broadcasted_iota(jnp.int32, (listed, total), 0)
+    wanted = (pair_lane // cap) % owners * owners + pair_lane // listed == pair_line
+
+    def along(field):
+        flat = metas_ref[:, field].reshape(listed, metas_ref.shape[3]).astype(jnp.bfloat16)
+        chosen = jnp.where(wanted, dot_nn(flat, spread), 0.0)
+        return jnp.sum(chosen, axis=0, keepdims=True)
+
+    key_y = along(0)
+    key_x = along(1)
     query_x = (
         lax.broadcasted_iota(jnp.int32, (lon_cells, total), 0) + lon * lon_cells
     ).astype(jnp.float32)
@@ -370,18 +428,10 @@
     ).astype(jnp.float32)
     off_y = key_y - query_y + float(REACH)
 
-    widened = jnp.concatenate([rows_ref[0], rows_ref[1]], axis=1)
-    wq_copy.wait_recv()
-    wk_copy.wait_recv()
-    wv_copy.wait_recv()
-    wo_copy.wait_recv()
-    head_copy.wait_recv()
     scale = 1.0 / math.sqrt(HEAD)
 
-    for wq, wk, wv, wo, per_head in (
-        (wq_ref, wk_ref, wv_ref, wo_ref, head_ref),
-        (wq2_ref, wk2_ref, wv2_ref, wo2_ref, head2_ref),
-    ):
+    def attend(wq, wk, wv, wo, per_head):
+        widened = jnp.concatenate([rows_ref[0], rows_ref[1]], axis=1)
         queries = (dot_nn(normed, wq[...]).astype(jnp.bfloat16) * scale).astype(jnp.bfloat16)
         keys = dot_nn(widened, wk[...]).astype(jnp.bfloat16)
         values = dot_nn(widened, wv[...]).astype(jnp.bfloat16)
@@ -428,19 +478,79 @@
 
         lax.fori_loop(0, heads, one_head, 0)
 
-    result = att_ref[...]
-    for step in range(1, n_lat):
-        part_copies[step - 1].wait_recv()
-        result = result + part_ref[step].astype(jnp.float32)
-    out_ref[...] = result.astype(jnp.bfloat16)
-
-    for copy in tok_copies + part_copies:
+    for hop in range(hops):
+        if hop == hops - 1:
+            back_rows.wait_recv()
+            attend(wq_ref, wk_ref, wv_ref, wo_ref, head_ref)
+        for way in ways:
+            source = lat - way * (1 + hop)
+
+            @pl.when(within(source))
+            def _():
+                tok_copy(way, hop, source).wait_recv()
+
+            @pl.when(within(source) & within(lat + way))
+            def _():
+                tok_copy(way, hop + 1, source).start()
+
+        for way in ways:
+            source = lat - way * (1 + hop)
+            at = (way > 0) * hops + hop
+
+            @pl.when(within(source))
+            def _():
+                back_ref[at] = fed(tok_ref[source])
+
+            @pl.when(within(source) & jnp.logical_not(within(lat + way)))
+            def _():
+                send_ref[at] = back_ref[at].astype(jnp.bfloat16)
+                sum_copy(way, hop).start()
+
+    for hop in range(hops - 2, -1, -1):
+        for way in ways:
+            source = lat - way * (1 + hop)
+            at = (way > 0) * hops + hop
+
+            @pl.when(within(source) & within(lat + way))
+            def _():
+                sum_copy(way, hop + 1).wait_recv()
+                total_here = back_ref[at] + part_ref[at + 1].astype(jnp.float32)
+                send_ref[at] = total_here.astype(jnp.bfloat16)
+                sum_copy(way, hop).start()
+
+    wq_copy.wait_recv()
+    wk_copy.wait_recv()
+    wv_copy.wait_recv()
+    wo_copy.wait_recv()
+    head_copy.wait_recv()
+    att_ref[...] += fed(normed)
+    attend(wq2_ref, wk2_ref, wv2_ref, wo2_ref, head2_ref)
+
+    for way in ways:
+
+        @pl.when(within(lat + way))
+        def _():
+            sum_copy(way, 0).wait_recv()
+            att_ref[...] += part_ref[(way > 0) * hops].astype(jnp.float32)
+
+    out_ref[...] = att_ref[...].astype(jnp.bfloat16)
+
+    for way in ways:
+        for hop in range(hops):
+
+            @pl.when(within(lat - way * hop) & within(lat + way))
+            def _():
+                tok_copy(way, hop, lat - way * hop).wait_send()
+
+            @pl.when(within(lat - way * (1 + hop)))
+            def _():
+                sum_copy(way, hop).wait_send()
+
+    for copy in pair_copies:
         copy.wait_send()
-    for copy in (up_copy, down_copy, wq_copy, wk_copy, wv_copy, wo_copy, head_copy):
-        copy.wait_send()
-    for step in range(1, group):
-        obs_copy(step, me).wait_send()
+    rows_copy.wait_send()
     for step in range(1, owners):
+        obs_copy(step, owner).wait_send()
         meta_copy(step, owner).wait_send()
 
 
@@ -464,101 +574,78 @@
     lat_cells, lon_cells, depth = latent.shape
     owners = n_lat * n_lon
     cap = bucket_slots.shape[2]
-    listed = observations.shape[0]
-    total = owners * listed
+    total = owners * owners * cap
     half_chan = observations.shape[1]
     heads = w_query.shape[1] // HEAD
     tokens = lat_cells * lon_cells // 2
     lanes = 128
-
-    slots = bucket_slots[0].reshape(-1)
-    row_slots = lon_cells * BUCKET
-    valid = slots < lat_cells * row_slots
-    cell_y = lax.axis_index("lat") * lat_cells + slots // row_slots
-    cell_x = lax.axis_index("lon") * lon_cells + (slots // BUCKET) % lon_cells
-    y_line = jnp.where(valid, cell_y.astype(jnp.float32), FAR)
-    x_line = jnp.where(valid, cell_x.astype(jnp.float32), 0.0)
-    count_line = send_counts[0].astype(jnp.float32)
-    meta = jnp.zeros((8, lanes), jnp.float32)
-    meta = jnp.concatenate(
-        [
-            jnp.pad(line, (0, lanes - line.shape[0]))[None]
-            for line in (y_line, x_line, count_line)
-        ]
-        + [jnp.zeros((5, lanes), jnp.float32)],
-        axis=0,
-    )
-    nulls = jnp.transpose(null_kv.astype(jnp.float32).reshape(2, heads, HEAD), (1, 0, 2))
-    per_head = jnp.concatenate(
-        [
-            jnp.pad(nulls, ((0, 0), (0, 0), (0, lanes - HEAD))),
-            jnp.pad(rel_bias, ((0, 0), (0, lanes - rel_bias.shape[1])))[:, None],
-            jnp.zeros((heads, 5, lanes), jnp.float32),
-        ],
-        axis=1,
-    )
-
-    lane = np.arange(total)
-    line = np.arange(lanes)
-    entry = np.arange(listed)
-    spread = line[:, None] == ((lane // (owners * cap)) * cap + lane % cap)[None]
-    own_lane = np.arange(owners)[:, None] == ((lane // cap) % owners)[None]
-    before = line[None] < (entry // cap)[:, None]
-    equal = line[None] == (entry // cap)[:, None]
-    places = np.broadcast_to((entry % cap)[:, None], (listed, lanes))
-
+    hops = n_lat - 1
     bf16 = jnp.bfloat16
     args = (
-        meta,
         observations,
-        jnp.asarray(spread, bf16),
-        jnp.asarray(own_lane, jnp.float32),
-        jnp.asarray(before, jnp.float32),
-        jnp.asarray(equal, jnp.float32),
-        jnp.asarray(places, jnp.float32),
-        latent.reshape(lat_cells * lon_cells, depth),
-        norm_gain.reshape(1, depth),
+        send_counts,
+        bucket_slots,
+        latent,
+        norm_gain,
         w_query,
         w_key,
         w_value,
-        per_head,
+        null_kv,
+        rel_bias,
         w_out,
         w_up,
         w_down,
     )
+    specs = [pl.BlockSpec(memory_space=pltpu.HBM)] * len(args)
+    specs[8] = pl.BlockSpec(memory_space=pltpu.VMEM)
+    head_shape = (heads, 8, lanes)
     dma = pltpu.SemaphoreType.DMA
-    group = 2 * owners
     out = pl.pallas_call(
         functools.partial(fused_kernel, (n_lat, n_lon, lat_cells, lon_cells, heads)),
         out_shape=jax.ShapeDtypeStruct((tokens, depth), bf16),
-        in_specs=[pl.BlockSpec(memory_space=pltpu.VMEM)] * len(args),
+        in_specs=specs,
         out_specs=pl.BlockSpec(memory_space=pltpu.VMEM),
         scratch_shapes=[
+            pltpu.VMEM(observations.shape, bf16),
+            pltpu.VMEM(send_counts.shape, jnp.int32),
+            pltpu.VMEM(bucket_slots.shape, jnp.int32),
+            pltpu.VMEM((lat_cells // 2, lon_cells, depth), bf16),
+            pltpu.VMEM(norm_gain.shape, jnp.float32),
             pltpu.VMEM(w_query.shape, bf16),
             pltpu.VMEM(w_key.shape, bf16),
             pltpu.VMEM(w_value.shape, bf16),
-            pltpu.VMEM(per_head.shape, jnp.float32),
+            pltpu.VMEM(rel_bias.shape, jnp.float32),
+            pltpu.VMEM(w_out.shape, bf16),
+            pltpu.VMEM(w_up.shape, bf16),
+            pltpu.VMEM(w_down.shape, bf16),
+            pltpu.VMEM(w_query.shape, bf16),
+            pltpu.VMEM(w_key.shape, bf16),
+            pltpu.VMEM(w_value.shape, bf16),
+            pltpu.VMEM(head_shape, jnp.float32),
+            pltpu.VMEM(head_shape, jnp.float32),
             pltpu.VMEM(w_out.shape, bf16),
             pltpu.VMEM(w_up.shape, bf16),
             pltpu.VMEM(w_down.shape, bf16),
             pltpu.VMEM((n_lat, tokens, depth), bf16),
-            pltpu.VMEM((n_lat, tokens, depth), bf16),
-            pltpu.VMEM((n_lat, tokens, depth), bf16),
+            pltpu.VMEM((2 * hops, tokens, depth), jnp.float32),
+            pltpu.VMEM((2 * hops, tokens, depth), bf16),
+            pltpu.VMEM((2 * hops, tokens, depth), bf16),
             pltpu.VMEM((2, total, half_chan), bf16),
-            pltpu.VMEM((owners,) + meta.shape, jnp.float32),
+            pltpu.VMEM((owners, 2, owners, lanes), jnp.float32),
             pltpu.VMEM((heads, tokens, HEAD), bf16),
             pltpu.VMEM((heads, total, HEAD), bf16),
             pltpu.VMEM((heads, total, HEAD), bf16),
             pltpu.VMEM((lon_cells, total), jnp.float32),
             pltpu.VMEM((tokens, depth), jnp.float32),
-            dma((7,)),
-            dma((7,)),
-            dma((n_lat,)),
-            dma((n_lat,)),
-            dma((n_lat,)),
-            dma((n_lat,)),
-            dma((group,)),
-            dma((group,)),
+            dma((12,)),
+            dma((8,)),
+            dma((8,)),
+            dma((2 * hops,)),
+            dma((2 * hops,)),
+            dma((2 * hops,)),
+            dma((2 * hops,)),
+            dma((owners,)),
+            dma((owners,)),
             dma((owners,)),
             dma((owners,)),
         ],
@@ -595,7 +682,7 @@
             n_rep == 2
             and n_lat in (2, 4)
             and listed <= 128
-            and observations.shape[0] == listed
+            and cap == n_lat * n_lon
         )
         step = functools.partial(fused, n_lat, n_lon) if direct else banded
         return step(observations, send_counts, bucket_slots, *rest)

time: 67.7 us -> 57.3 us (0.85)
  Pallas kernels: 51.5 us -> 44.8 us
  local copies, waits for them, and re-layouts: 14.5 us -> 11.9 us
  other arithmetic: 0.87 us -> 0 us
    pallas_call x1, Pallas kernels: 51.5 us -> 44.8 us  [fused(): pl.pallas_call(functools.partial(fused_kernel, (n_lat, n_lon, lat_cells,...]
    reshape x3 -> x0, local copies, waits for them, and re-layouts: 1.46 us -> none  [the longest x2 0.77 us: fused(): null_kv.astype(jnp.float32).reshape(2, heads, HEAD)]
    another operation x1 -> x0, local copies, waits for them, and re-layouts: 0.76 us -> none  [fused(): slots = bucket_slots[0].reshape(-1)]
    pad x1 -> x0, local copies, waits for them, and re-layouts: 0.69 us -> none  [fused(): jnp.pad(rel_bias, ((0, 0), (0, lanes - rel_bias.shape[1])))[:, None]]
    convert_element_type x1 -> x0, other arithmetic: 0.69 us -> none  [fused(): count_line = send_counts[0].astype(jnp.float32)]
where the time goes in v2:
time: 57.3 us; the launch traced here: 56.7 us
  Pallas kernels  44.8 us (78%)
  local copies, waits for them, and re-layouts  11.9 us (21%)
    pallas_call x1, Pallas kernels, fused(): pl.pallas_call(functools.partial(fused_kernel, (n_lat, n_lon, lat_cells,...  44.8 us
    unnamed x27, local copies, waits for them, and re-layouts  11.9 us

profile of v2, /device:TPU:0, one launch (start us, length us, event | category | flops | bytes accessed | tf_op | source)
XLA Modules:
  0.0 56.7 jit_solution(17243461224889053027)
XLA Ops:
  0.0 0.0 copy-start
  0.0 1.1 %copy-done = bf16[768,384]{1,0:T(8,128)(2,1)S(1)} copy-done((bf16[768,384]{1,0:T(8,128)(2,1)S(1)}, bf16[768,384]{1,0:T(8,128)(2,1)}, u32[]{:S(2)}) %copy-start) | copy-done | bytes 589848
  1.1 0.0 copy-start.1
  1.1 1.1 %copy-done.1 = bf16[384,768]{1,0:T(8,128)(2,1)S(1)} copy-done((bf16[384,768]{1,0:T(8,128)(2,1)S(1)}, bf16[384,768]{1,0:T(8,128)(2,1)}, u32[]{:S(2)}) %copy-start.1) | copy-done | bytes 589848
  2.1 0.0 copy-start.2
  2.1 1.1 %copy-done.2 = bf16[384,768]{1,0:T(8,128)(2,1)S(1)} copy-done((bf16[384,768]{1,0:T(8,128)(2,1)S(1)}, bf16[384,768]{1,0:T(8,128)(2,1)}, u32[]{:S(2)}) %copy-start.2) | copy-done | bytes 589848
  3.2 0.0 copy-start.3
  3.2 1.1 %copy-done.3 = bf16[384,768]{1,0:T(8,128)(2,1)S(1)} copy-done((bf16[384,768]{1,0:T(8,128)(2,1)S(1)}, bf16[384,768]{1,0:T(8,128)(2,1)}, u32[]{:S(2)}) %copy-start.3) | copy-done | bytes 589848
  4.3 0.0 copy-start.4
  4.3 1.0 %copy-done.4 = bf16[8,32,768]{2,1,0:T(8,128)(2,1)S(1)} copy-done((bf16[8,32,768]{2,1,0:T(8,128)(2,1)S(1)}, bf16[8,32,768]{2,1,0:T(8,128)(2,1)}, u32[]{:S(2)}) %copy-start.4) | copy-done | bytes 393240
  5.3 0.0 copy-start.5
  5.3 0.9 %copy-done.5 = bf16[256,384]{1,0:T(8,128)(2,1)S(1)} copy-done((bf16[256,384]{1,0:T(8,128)(2,1)S(1)}, bf16[256,384]{1,0:T(8,128)(2,1)}, u32[]{:S(2)}) %copy-start.5) | copy-done | bytes 196632
  6.2 0.0 copy-start.6
  6.2 0.9 %copy-done.6 = bf16[256,384]{1,0:T(8,128)(2,1)S(1)} copy-done((bf16[256,384]{1,0:T(8,128)(2,1)S(1)}, bf16[256,384]{1,0:T(8,128)(2,1)}, u32[]{:S(2)}) %copy-start.6) | copy-done | bytes 196632
  7.1 0.0 copy-start.7
  7.1 0.7 %copy-done.7 = bf16[64,128]{1,0:T(8,128)(2,1)S(1)} copy-done((bf16[64,128]{1,0:T(8,128)(2,1)S(1)}, bf16[64,128]{1,0:T(8,128)(2,1)}, u32[]{:S(2)}) %copy-start.7) | copy-done | bytes 16408
  7.8 0.0 copy-start.8
  7.8 0.7 %copy-done.8 = s32[1,8,8]{2,1,0:T(8,128)S(1)} copy-done((s32[1,8,8]{2,1,0:T(8,128)S(1)}, s32[1,8,8]{2,1,0:T(8,128)}, u32[]{:S(2)}) %copy-start.8) | copy-done | bytes 280
  8.5 0.7 %copy-done.9 = f32[768]{0:T(1024)S(1)} copy-done((f32[768]{0:T(1024)S(1)}, f32[768]{0:T(1024)}, u32[]{:S(2)}) %copy-start.9) | copy-done | bytes 3096
  9.2 0.7 %copy-done.10 = f32[6,25]{1,0:T(8,128)S(1)} copy-done((f32[6,25]{1,0:T(8,128)S(1)}, f32[6,25]{1,0:T(8,128)}, u32[]{:S(2)}) %copy-start.10) | copy-done | bytes 624
  9.9 0.7 %copy-done.11 = bf16[2,384]{1,0:T(2,128)(2,1)S(1)} copy-done((bf16[2,384]{1,0:T(2,128)(2,1)S(1)}, bf16[2,384]{1,0:T(2,128)(2,1)}, u32[]{:S(2)}) %copy-start.11) | copy-done | bytes 1560
  10.6 0.7 %copy-done.12 = s32[1,8]{1,0:T(1,128)S(1)} copy-done((s32[1,8]{1,0:T(1,128)S(1)}, s32[1,8]{1,0:T(1,128)}, u32[]{:S(2)}) %copy-start.12) | copy-done | bytes 56
  11.2 44.8 %shard_map.127 = bf16[128,768]{1,0:T(8,128)(2,1)S(1)} custom-call(bf16[64,128]{1,0:T(8,128)(2,1)S(1)} %copy-done.7, s32[1,8]{1,0:T(1,128)S(1)} %copy-done.12, s32[1,8,8]{2,1,0:T(8,128)S(1)} %copy-done.8, bf16[8,32,768]{2,1,0:T(8,128)(2,1)S(1)} %copy-done.4, f32[768]{0:T(1024)S(1)} %copy-done.9, bf16[768,384]{1,0:T(8,128)(2,1)S(1)} %copy-done, ...), custom_call_target="tpu_custom_call" | custom-call | tf_op jit(solution)/shard_map/pallas_call | solution.py:603
  56.1 0.7 %copy.15 = bf16[4,32,768]{2,1,0:T(8,128)(2,1)} copy(bf16[4,32,768]{2,1,0:T(8,128)(2,1)S(1)} %bitcast.1) | data formatting | bytes 393216
  (4 shorter events, 0.0 us)
Async XLA Ops:
  0.0 1.1 %copy-start = (bf16[768,384]{1,0:T(8,128)(2,1)S(1)}, bf16[768,384]{1,0:T(8,128)(2,1)}, u32[]{:S(2)}) copy-start(bf16[768,384]{1,0:T(8,128)(2,1)} %wq_hbm.1) | copy-start | bytes 1769476
  1.1 1.1 %copy-start.1 = (bf16[384,768]{1,0:T(8,128)(2,1)S(1)}, bf16[384,768]{1,0:T(8,128)(2,1)}, u32[]{:S(2)}) copy-start(bf16[384,768]{1,0:T(8,128)(2,1)} %wo_hbm.1) | copy-start | bytes 1769476
  2.1 1.1 %copy-start.2 = (bf16[384,768]{1,0:T(8,128)(2,1)S(1)}, bf16[384,768]{1,0:T(8,128)(2,1)}, u32[]{:S(2)}) copy-start(bf16[384,768]{1,0:T(8,128)(2,1)} %up_hbm.1) | copy-start | bytes 1769476
  3.2 1.1 %copy-start.3 = (bf16[384,768]{1,0:T(8,128)(2,1)S(1)}, bf16[384,768]{1,0:T(8,128)(2,1)}, u32[]{:S(2)}) copy-start(bf16[384,768]{1,0:T(8,128)(2,1)} %down_hbm.1) | copy-start | bytes 1769476
  4.3 1.0 %copy-start.4 = (bf16[8,32,768]{2,1,0:T(8,128)(2,1)S(1)}, bf16[8,32,768]{2,1,0:T(8,128)(2,1)}, u32[]{:S(2)}) copy-start(bf16[8,32,768]{2,1,0:T(8,128)(2,1)} %lat_hbm.1) | copy-start | bytes 1179652
  5.3 0.9 %copy-start.5 = (bf16[256,384]{1,0:T(8,128)(2,1)S(1)}, bf16[256,384]{1,0:T(8,128)(2,1)}, u32[]{:S(2)}) copy-start(bf16[256,384]{1,0:T(8,128)(2,1)} %wk_hbm.1) | copy-start | bytes 589828
  6.2 0.9 %copy-start.6 = (bf16[256,384]{1,0:T(8,128)(2,1)S(1)}, bf16[256,384]{1,0:T(8,128)(2,1)}, u32[]{:S(2)}) copy-start(bf16[256,384]{1,0:T(8,128)(2,1)} %wv_hbm.1) | copy-start | bytes 589828
  7.1 0.7 %copy-start.7 = (bf16[64,128]{1,0:T(8,128)(2,1)S(1)}, bf16[64,128]{1,0:T(8,128)(2,1)}, u32[]{:S(2)}) copy-start(bf16[64,128]{1,0:T(8,128)(2,1)} %obs_hbm.1) | copy-start | bytes 49156
  7.8 0.7 %copy-start.8 = (s32[1,8,8]{2,1,0:T(8,128)S(1)}, s32[1,8,8]{2,1,0:T(8,128)}, u32[]{:S(2)}) copy-start(s32[1,8,8]{2,1,0:T(8,128)} %slots_hbm.1) | copy-start | bytes 772
  8.5 0.7 %copy-start.9 = (f32[768]{0:T(1024)S(1)}, f32[768]{0:T(1024)}, u32[]{:S(2)}) copy-start(f32[768]{0:T(1024)} %gain_hbm.1) | copy-start | bytes 9220
  9.2 0.7 %copy-start.10 = (f32[6,25]{1,0:T(8,128)S(1)}, f32[6,25]{1,0:T(8,128)}, u32[]{:S(2)}) copy-start(f32[6,25]{1,0:T(8,128)} %bias_hbm.1) | copy-start | bytes 1804
  9.9 0.7 %copy-start.11 = (bf16[2,384]{1,0:T(2,128)(2,1)S(1)}, bf16[2,384]{1,0:T(2,128)(2,1)}, u32[]{:S(2)}) copy-start(bf16[2,384]{1,0:T(2,128)(2,1)} %null_ref.1) | copy-start | bytes 4612
  10.6 0.7 %copy-start.12 = (s32[1,8]{1,0:T(1,128)S(1)}, s32[1,8]{1,0:T(1,128)}, u32[]{:S(2)}) copy-start(s32[1,8]{1,0:T(1,128)} %counts_hbm.1) | copy-start | bytes 100
